TPU v7x, 256 devices: a whole 4x4x8 slice. The times are simulated.
256 devices in a mesh: member: 64 (over y, z, core), slab: 4 (over x).
Axes of the slice: x: 4, y: 4, z: 8, core: 2. Of those that a mesh axis runs over, the one named last changes fastest.
Arguments:
- ensemble_obs: bfloat16 [512, 4, 32768], P('member', 'slab'), may hold values from -6 to 6
- obs_values: bfloat16 [2, 4, 32768], P(None, 'slab', 'member'), may hold values from -9 to 9
- obs_index: int32 [4, 128, 512], P('slab', 'member'), may hold values from 0 to 1023, as said below
- obs_count: int32 [4, 128], P('slab', 'member'), may hold values from 1 to 512, as said below
- loc_weight: float32 [4, 128, 512], P('slab', 'member'), may hold values from 0.05 to 1
- state: bfloat16 [512, 4, 128, 2048], P('member', 'slab'), may hold values from -6 to 6
Outputs:
- analysis: bfloat16 [512, 4, 128, 2048], P('member', 'slab')
Inputs may be any that keep to these rules, and one draw needn't show every extreme that they name: `obs_index`: each block's first slot holds position 0 for even block numbers and 1023 for odd ones. `obs_count`: every strip has a block that uses all 512 slots.
All inputs are finite; a program needn't handle non-finite values.
Results may differ from a plain program's by a relative error of at most 0.019.
Values may be sent and summed in bfloat16 or wider, within the bound.
A program may use at most 64 MiB of HBM per device.

v0:
```python
import functools

import jax
import jax.numpy as jnp
from jax import lax
from jax.experimental import pallas as pl
from jax.experimental.pallas import tpu as pltpu
from jax.sharding import PartitionSpec as P

MESH = pl.DeviceIdType.MESH
F32 = jnp.float32
BF16 = jnp.bfloat16
HIGHEST = lax.Precision.HIGHEST

PEERS = 64
SLABS = 4
ROWS = 8
K = 512
BLKS = 2
MSG = BLKS * ROWS
CELLS = 2048
PIECES = 4
W = CELLS // PIECES
RIM = 256
POOL = 1024
GROUP = 8
GROUPS = PEERS // GROUP


def nt(a, b, precision=None):
    return lax.dot_general(
        a, b, (((1,), (1,)), ((), ())), precision=precision, preferred_element_type=F32
    )


def mm(a, b):
    return jnp.dot(a, b, precision=HIGHEST, preferred_element_type=F32)


def iota(shape, axis):
    return lax.broadcasted_iota(jnp.int32, shape, axis)


def split3(row, width):
    full = jnp.broadcast_to(row, (16, width))
    high = full.astype(BF16).astype(F32)
    rest = full - high
    mid = rest.astype(BF16).astype(F32)
    low = rest - mid
    r = iota((16, width), 0)
    rows = jnp.where(r == 0, high, jnp.where(r == 1, mid, jnp.where(r == 2, low, 0.0)))
    return rows.astype(BF16)


def gather_rows(inverse):
    n = GROUP * MSG
    out, src = iota((n, n), 0), iota((n, n), 1)
    if inverse:
        out, src = src, out
    wanted = (out % ROWS) * MSG + out // ROWS
    return jnp.where(src == wanted, 1.0, 0.0).astype(BF16)


def exchange(
    state, obs, vals, idx, cnt, loc, back,
    stage, fsend, frecv, bsend, osend, orecv, hsend, hrecv,
    pert, wgt, mats, expand, tbigf, tbig, spert,
    st_sem, fs_sem, fr_sem, fl_sem, bs_sem, br_sem, bl_sem,
    os_sem, or_sem, ol_sem, hs_sem, hr_sem,
):
    me = lax.axis_index("member")
    slab = lax.axis_index("slab")
    right = lax.rem(slab + 1, SLABS)
    left = lax.rem(slab + SLABS - 1, SLABS)

    barrier = pltpu.get_barrier_semaphore()

    def greet(i, carry):
        pl.semaphore_signal(
            barrier, inc=1, device_id={"member": lax.rem(me + 27 * i, PEERS)}, device_id_type=MESH
        )
        return carry

    lax.fori_loop(1, PEERS, greet, 0)
    for neighbour in (left, right):
        pl.semaphore_signal(barrier, inc=1, device_id={"slab": neighbour}, device_id_type=MESH)

    def stage_copy(p):
        cols = pl.ds(p * W, W)
        return pltpu.make_async_copy(
            state.at[:, 0, :, cols], stage.at[:, :, cols], st_sem.at[p]
        )

    for p in range(PIECES):
        stage_copy(p).start()

    def fill_obs(r, carry):
        a = obs[:, pl.ds(pl.multiple_of(r * 2 * RIM, 2 * RIM), RIM)].astype(F32)
        b = obs[:, pl.ds(pl.multiple_of(r * 2 * RIM + RIM, RIM), RIM)].astype(F32)
        osend[r] = jnp.concatenate([a, b], axis=0).astype(BF16)
        return carry

    lax.fori_loop(0, PEERS, fill_obs, 0)
    pl.semaphore_wait(barrier, PEERS - 1 + 2)

    own_obs = pltpu.make_async_copy(osend.at[me], orecv.at[me], ol_sem)
    own_obs.start()

    def send_obs(i, carry):
        d = lax.rem(me + 27 * i, PEERS)
        pltpu.make_async_remote_copy(
            src_ref=osend.at[d], dst_ref=orecv.at[me], send_sem=os_sem, recv_sem=or_sem,
            device_id={"member": d}, device_id_type=MESH,
        ).start()
        return carry

    lax.fori_loop(1, PEERS, send_obs, 0)

    def forward(p):
        stage_copy(p).wait()
        cols = pl.ds(p * W, W)

        def group(i, carry):
            g = lax.rem(me // GROUP + i, GROUPS)
            first = pl.multiple_of(g * GROUP, GROUP)
            rows = stage[:, pl.ds(pl.multiple_of(g * MSG, MSG), MSG), cols]
            moved = jnp.dot(
                gather_rows(False), rows.reshape(GROUP * MSG, W), preferred_element_type=F32
            )
            fsend[p, pl.ds(first, GROUP)] = moved.astype(BF16).reshape(GROUP, MSG, W)

            def one(j, inner):
                d = first + j

                @pl.when(d != me)
                def _():
                    pltpu.make_async_remote_copy(
                        src_ref=fsend.at[p, d], dst_ref=frecv.at[p, me],
                        send_sem=fs_sem.at[p], recv_sem=fr_sem.at[p],
                        device_id={"member": d}, device_id_type=MESH,
                    ).start()

                return inner

            lax.fori_loop(0, GROUP, one, 0)
            return carry

        lax.fori_loop(0, GROUPS, group, 0)
        pltpu.make_async_copy(fsend.at[p, me], frecv.at[p, me], fl_sem.at[p]).start()

    forward(0)

    own_obs.wait()
    most = pl.ds(0, PEERS - 1)
    pltpu.make_async_copy(osend.at[most], orecv.at[most], or_sem).wait()

    def halves(i, carry):
        x = orecv[pl.ds(i * 8, 8)].astype(F32)
        rows = pl.ds(pl.multiple_of(i * 64, 64), 64)
        hsend[1, rows] = x[:, :ROWS].reshape(64, RIM).astype(BF16)
        hsend[0, rows] = x[:, ROWS:].reshape(64, RIM).astype(BF16)
        return carry

    lax.fori_loop(0, 8, halves, 0)
    v = vals[...].astype(F32)
    for side, at in ((1, 0), (0, RIM)):
        r = iota((16, RIM), 0)
        first, second = v[0:1, at : at + RIM], v[1:2, at : at + RIM]
        hsend[side, K : K + 16] = jnp.where(
            r == 0, first, jnp.where(r == 1, second, 0.0)
        ).astype(BF16)
    halos = [
        pltpu.make_async_remote_copy(
            src_ref=hsend.at[side], dst_ref=hrecv.at[side],
            send_sem=hs_sem.at[side], recv_sem=hr_sem.at[side],
            device_id={"slab": to}, device_id_type=MESH,
        )
        for side, to in ((0, right), (1, left))
    ]
    for halo in halos:
        halo.start()

    for p in range(1, PIECES):
        forward(p)

    def fill_expand(i, carry):
        j = iota((64, POOL), 0) + i * 64
        c = iota((64, POOL), 1)
        rows = pl.ds(pl.multiple_of(i * 64, 64), 64)
        for b in range(BLKS):
            at = (j // ROWS) * MSG + b * ROWS + j % ROWS
            expand[b, rows] = jnp.where(c == at, 1.0, 0.0).astype(BF16)
        return carry

    lax.fori_loop(0, K // 64, fill_expand, 0)

    for halo in halos:
        halo.wait()

    departs, inverses = [], []
    for q, ref in enumerate((hrecv.at[0], hsend.at[1], hsend.at[0], hrecv.at[1])):
        x = ref[:K].astype(F32)
        mean = jnp.sum(x, axis=0, keepdims=True) * (1.0 / K)
        pert[:, q * RIM : (q + 1) * RIM] = (x - mean).astype(BF16)
        tail = ref[K : K + 16].astype(F32)
        departs.append(tail[0:1] - mean)
        inverses.append(tail[1:2])
    depart = split3(jnp.concatenate(departs, axis=1), POOL)

    diagonal = iota((K, K), 0) == iota((K, K), 1)
    for b in range(BLKS):
        row = idx[b : b + 1, :]
        slot = iota((1, 512), 1)
        local = jnp.where(slot < cnt[0, b], loc[b : b + 1, :], 0.0)
        local = split3(local, 512)
        for q in range(4):
            hit = iota((RIM, 512), 0) + q * RIM == row
            hit = jnp.where(hit, 1.0, 0.0).astype(BF16)
            total = nt(local, hit)
            weight = inverses[q] * (total[0:1] + total[1:2] + total[2:3])
            cols = slice(q * RIM, (q + 1) * RIM)
            wgt[b, :, cols] = (pert[:, cols].astype(F32) * weight).astype(BF16)

    def transform(b, carry):
        weighted = wgt[b]
        drive = nt(depart, weighted)
        drive = jnp.broadcast_to(drive[0:1] + drive[1:2] + drive[2:3], (8, K))
        gram = nt(pert[...], weighted) + jnp.where(diagonal, K - 1.0, 0.0)
        scale = jnp.sum(gram * gram, axis=1, keepdims=True)
        scale = jnp.sqrt(jnp.sum(scale, axis=0, keepdims=True))
        matrix = gram * (1.0 / scale)
        factor = jnp.where(diagonal, 1.5, 0.0) - 0.5 * matrix
        mats[1] = factor
        mats[0] = mm(matrix, factor)
        mats[2] = jnp.where(diagonal, 1.5, 0.0) - 0.5 * mm(mats[1], mats[0])
        mats[0] = mm(mats[0], mats[2])
        mats[1] = mm(mats[2], mats[1])
        mats[2] = jnp.where(diagonal, 1.5, 0.0) - 0.5 * mm(mats[1], mats[0])
        mats[0] = mm(mats[2], mats[1])
        inverse = mats[0]
        inner = nt(drive, inverse, HIGHEST)
        shift = nt(inner, inverse, HIGHEST)[0:1] / scale
        spread = jnp.sqrt((K - 1.0) / scale)
        mats[1] = spread * inverse.T + shift

        def widen(i, inner_carry):
            rows = mats[1, pl.ds(pl.multiple_of(i * 128, 128), 128)].astype(BF16)
            wide = jnp.dot(rows, expand[b], preferred_element_type=F32)
            at = pl.ds(pl.multiple_of(b * ROWS, ROWS), ROWS)
            tbigf[pl.ds(i * 16, 16), at] = wide.reshape(16, ROWS, POOL)
            return inner_carry

        lax.fori_loop(0, 4, widen, 0)
        return carry

    lax.fori_loop(0, BLKS, transform, 0)

    def narrow(i, carry):
        rows = pl.ds(pl.multiple_of(i * 128, 128), 128)
        tbig[rows] = tbigf[pl.ds(i * 8, 8)].reshape(128, POOL).astype(BF16)
        return carry

    lax.fori_loop(0, 8, narrow, 0)

    for p in range(PIECES):
        pltpu.make_async_copy(fsend.at[p, me], frecv.at[p, me], fl_sem.at[p]).wait()
        pltpu.make_async_copy(fsend.at[p, most], frecv.at[p, most], fr_sem.at[p]).wait()

        def add_up(i, total):
            x = frecv[p, pl.ds(i * 4, 4)].astype(F32)
            return total + jnp.sum(x, axis=0)

        total = lax.fori_loop(0, 16, add_up, jnp.zeros((MSG, W), F32))
        means = [
            jnp.sum(total[b * ROWS : (b + 1) * ROWS], axis=0, keepdims=True) * (1.0 / K)
            for b in range(BLKS)
        ]
        mean = jnp.concatenate([jnp.broadcast_to(m, (ROWS, W)) for m in means], axis=0)

        def less_mean(i, carry):
            x = frecv[p, pl.ds(i * 4, 4)].astype(F32) - mean[None]
            spert[pl.ds(pl.multiple_of(i * 64, 64), 64)] = x.reshape(64, W).astype(BF16)
            return carry

        lax.fori_loop(0, 16, less_mean, 0)

        def apply(i, carry):
            part = lax.rem(me // 16 + i, 4)
            rows = tbig[pl.ds(pl.multiple_of(part * 256, 256), 256)]
            moved = jnp.dot(rows, spert[...], preferred_element_type=F32)
            new = moved.reshape(16, MSG, W) + mean[None]
            first = pl.multiple_of(part * 16, 16)
            bsend[p, pl.ds(first, 16)] = new.astype(BF16)

            def one(j, inner):
                d = first + lax.rem(j * 7 + me, 16)

                @pl.when(d != me)
                def _():
                    pltpu.make_async_remote_copy(
                        src_ref=bsend.at[p, d], dst_ref=back.at[p, me],
                        send_sem=bs_sem.at[p], recv_sem=br_sem.at[p],
                        device_id={"member": d}, device_id_type=MESH,
                    ).start()

                return inner

            lax.fori_loop(0, 16, one, 0)
            return carry

        lax.fori_loop(0, 4, apply, 0)
        pltpu.make_async_copy(bsend.at[p, me], back.at[p, me], bl_sem.at[p]).start()

    pltpu.make_async_copy(osend.at[most], orecv.at[most], os_sem).wait()
    for p in range(PIECES):
        pltpu.make_async_copy(fsend.at[p, most], frecv.at[p, most], fs_sem.at[p]).wait()
        pltpu.make_async_copy(bsend.at[p, most], back.at[p, most], bs_sem.at[p]).wait()
        pltpu.make_async_copy(bsend.at[p, me], back.at[p, me], bl_sem.at[p]).wait()
        pltpu.make_async_copy(bsend.at[p, most], back.at[p, most], br_sem.at[p]).wait()


def put_back(parts, out):
    order = gather_rows(True)
    for p in range(PIECES):
        rows = parts[p].reshape(GROUP * MSG, W)
        moved = jnp.dot(order, rows, preferred_element_type=F32).astype(BF16)
        out[:, 0, :, p * W : (p + 1) * W] = moved.reshape(ROWS, MSG, W)


def on_device(ensemble_obs, obs_values, obs_index, obs_count, loc_weight, state):
    any_space = pl.BlockSpec(memory_space=pl.ANY)
    vmem = pl.BlockSpec(memory_space=pltpu.VMEM)
    smem = pl.BlockSpec(memory_space=pltpu.SMEM)
    dma = pltpu.SemaphoreType.DMA
    back = pl.pallas_call(
        exchange,
        name="exchange",
        out_shape=jax.ShapeDtypeStruct((PIECES, PEERS, MSG, W), BF16),
        in_specs=[any_space, vmem, vmem, vmem, smem, vmem],
        out_specs=any_space,
        scratch_shapes=[
            pltpu.VMEM((ROWS, PEERS * BLKS, CELLS), BF16),
            pltpu.VMEM((PIECES, PEERS, MSG, W), BF16),
            pltpu.VMEM((PIECES, PEERS, MSG, W), BF16),
            pltpu.VMEM((PIECES, PEERS, MSG, W), BF16),
            pltpu.VMEM((PEERS, MSG, RIM), BF16),
            pltpu.VMEM((PEERS, MSG, RIM), BF16),
            pltpu.VMEM((2, K + 16, RIM), BF16),
            pltpu.VMEM((2, K + 16, RIM), BF16),
            pltpu.VMEM((K, POOL), BF16),
            pltpu.VMEM((BLKS, K, POOL), BF16),
            pltpu.VMEM((3, K, K), F32),
            pltpu.VMEM((BLKS, K, POOL), BF16),
            pltpu.VMEM((PEERS, MSG, POOL), F32),
            pltpu.VMEM((BLKS * K, BLKS * K), BF16),
            pltpu.VMEM((BLKS * K, W), BF16),
            dma((PIECES,)), dma((PIECES,)), dma((PIECES,)), dma((PIECES,)),
            dma((PIECES,)), dma((PIECES,)), dma((PIECES,)),
            dma, dma, dma, dma((2,)), dma((2,)),
        ],
        compiler_params=pltpu.CompilerParams(
            collective_id=0, has_side_effects=True, vmem_limit_bytes=56 << 20
        ),
    )(
        state,
        ensemble_obs.reshape(ROWS, PEERS * 2 * RIM),
        obs_values.reshape(2, 2 * RIM),
        obs_index.reshape(BLKS, 512),
        obs_count,
        loc_weight.reshape(BLKS, 512),
    )
    return pl.pallas_call(
        put_back,
        name="put_back",
        grid=(GROUPS,),
        out_shape=jax.ShapeDtypeStruct(state.shape, BF16),
        in_specs=[pl.BlockSpec((PIECES, GROUP, MSG, W), lambda g: (0, g, 0, 0))],
        out_specs=pl.BlockSpec((ROWS, 1, MSG, CELLS), lambda g: (0, 0, g, 0)),
    )(back)


def solution(mesh):
    placed = (
        P("member", "slab", None),
        P(None, "slab", "member"),
        P("slab", "member", None),
        P("slab", "member"),
        P("slab", "member", None),
        P("member", "slab", None, None),
    )
    return jax.shard_map(
        on_device,
        mesh=mesh,
        in_specs=placed,
        out_specs=P("member", "slab", None, None),
        check_vma=False,
    )
```

profile of v0, /device:TPU:1, one launch (start us, length us, event | category | flops | bytes accessed | tf_op | source)
XLA Modules:
  0.0 213.8 jit_solution(4271445060104562152)
XLA Ops:
  0.0 206.3 %exchange.1.parts = bf16[4,64,16,512]{3,2,1,0:T(8,128)(2,1)} custom-call(bf16[8,1,128,2048]{3,2,1,0:T(8,128)(2,1)} %state.1, bf16[8,32768]{1,0:T(8,128)(2,1)} %bitcast.4, bf16[2,512]{1,0:T(2,128)(2,1)} %bitcast.7, s32[2,512]{1,0:T(2,128)} %bitcast.5, s32[1,2]{1,0:T(1,128)} %cnt.1, f32[2,512]{1,0:T(2,128)} %bitcast.6), custom_call_target="tpu_custom_call" | custom-call | tf_op jit(solution)/shard_map/exchange/pallas_call | solution.py:335
  206.3 7.5 %put_back.1 = bf16[8,1,128,2048]{3,2,1,0:T(8,128)(2,1)} custom-call(bf16[4,64,16,512]{3,2,1,0:T(8,128)(2,1)} %exchange.1.parts), custom_call_target="tpu_custom_call" | custom-call | tf_op jit(solution)/shard_map/put_back/pallas_call | solution.py:372
where the time goes:
time: 214 us
  Pallas kernels  214 us (100%)
    pallas_call x1, Pallas kernels, on_device(): pl.pallas_call(exchange, name='exchange', out_shape=jax.ShapeDtypeStruct(...  206 us
    pallas_call x1, Pallas kernels, on_device(): pl.pallas_call(put_back, name='put_back', grid=(GROUPS,), out_shape=jax.S...  7.48 us

commit v1 on v0

--- a/solution.py
+++ b/solution.py
@@ -62,10 +62,10 @@
 
 
 def exchange(
-    state, obs, vals, idx, cnt, loc, back,
-    stage, fsend, frecv, bsend, osend, orecv, hsend, hrecv,
+    state, obs_in, vals_in, idx_in, cnt_in, loc_in, out,
+    obs, vals, idx, loc, cnt, stage, fsend, frecv, bsend, back, osend, orecv, hsend, hrecv,
     pert, wgt, mats, expand, tbigf, tbig, spert,
-    st_sem, fs_sem, fr_sem, fl_sem, bs_sem, br_sem, bl_sem,
+    in_sem, st_sem, fs_sem, fr_sem, fl_sem, bs_sem, br_sem,
     os_sem, or_sem, ol_sem, hs_sem, hr_sem,
 ):
     me = lax.axis_index("member")
@@ -81,9 +81,18 @@
         )
         return carry
 
-    lax.fori_loop(1, PEERS, greet, 0)
+    lax.fori_loop(1, PEERS, greet, 0, unroll=7)
     for neighbour in (left, right):
         pl.semaphore_signal(barrier, inc=1, device_id={"slab": neighbour}, device_id_type=MESH)
+
+    fetches = [
+        pltpu.make_async_copy(source, target, in_sem.at[n])
+        for n, (source, target) in enumerate(
+            ((obs_in, obs), (vals_in, vals), (idx_in, idx), (loc_in, loc), (cnt_in, cnt))
+        )
+    ]
+    for fetch in fetches:
+        fetch.start()
 
     def stage_copy(p):
         cols = pl.ds(p * W, W)
@@ -93,21 +102,17 @@
 
     for p in range(PIECES):
         stage_copy(p).start()
-
-    def fill_obs(r, carry):
+    fetches[0].wait()
+    pl.semaphore_wait(barrier, PEERS - 1 + 2)
+
+    def message(r):
         a = obs[:, pl.ds(pl.multiple_of(r * 2 * RIM, 2 * RIM), RIM)].astype(F32)
         b = obs[:, pl.ds(pl.multiple_of(r * 2 * RIM + RIM, RIM), RIM)].astype(F32)
         osend[r] = jnp.concatenate([a, b], axis=0).astype(BF16)
-        return carry
-
-    lax.fori_loop(0, PEERS, fill_obs, 0)
-    pl.semaphore_wait(barrier, PEERS - 1 + 2)
-
-    own_obs = pltpu.make_async_copy(osend.at[me], orecv.at[me], ol_sem)
-    own_obs.start()
 
     def send_obs(i, carry):
         d = lax.rem(me + 27 * i, PEERS)
+        message(d)
         pltpu.make_async_remote_copy(
             src_ref=osend.at[d], dst_ref=orecv.at[me], send_sem=os_sem, recv_sem=or_sem,
             device_id={"member": d}, device_id_type=MESH,
@@ -115,6 +120,11 @@
         return carry
 
     lax.fori_loop(1, PEERS, send_obs, 0)
+    message(me)
+    own_obs = pltpu.make_async_copy(osend.at[me], orecv.at[me], ol_sem)
+    own_obs.start()
+    for fetch in fetches[1:]:
+        fetch.wait()
 
     def forward(p):
         stage_copy(p).wait()
@@ -299,7 +309,7 @@
                 def _():
                     pltpu.make_async_remote_copy(
                         src_ref=bsend.at[p, d], dst_ref=back.at[p, me],
-                        send_sem=bs_sem.at[p], recv_sem=br_sem.at[p],
+                        send_sem=bs_sem.at[p], recv_sem=br_sem.at[p, me // GROUP],
                         device_id={"member": d}, device_id_type=MESH,
                     ).start()
 
@@ -309,74 +319,81 @@
             return carry
 
         lax.fori_loop(0, 4, apply, 0)
-        pltpu.make_async_copy(bsend.at[p, me], back.at[p, me], bl_sem.at[p]).start()
+        pltpu.make_async_copy(bsend.at[p, me], back.at[p, me], br_sem.at[p, me // GROUP]).start()
+
+    for p in range(PIECES):
+
+        def place(i, carry):
+            y = lax.rem(me // 16 + 4 - i // 2, 4)
+            g = y * 2 + lax.rem(i, 2)
+            some = pl.ds(pl.multiple_of(g * GROUP, GROUP), GROUP)
+            pltpu.make_async_copy(bsend.at[p, some], back.at[p, some], br_sem.at[p, g]).wait()
+            moved = jnp.dot(
+                gather_rows(True), back[p, some].reshape(GROUP * MSG, W), preferred_element_type=F32
+            )
+            rows = pl.ds(pl.multiple_of(g * MSG, MSG), MSG)
+            out[:, 0, rows, p * W : (p + 1) * W] = moved.astype(BF16).reshape(ROWS, MSG, W)
+            return carry
+
+        lax.fori_loop(0, GROUPS, place, 0)
 
     pltpu.make_async_copy(osend.at[most], orecv.at[most], os_sem).wait()
     for p in range(PIECES):
         pltpu.make_async_copy(fsend.at[p, most], frecv.at[p, most], fs_sem.at[p]).wait()
         pltpu.make_async_copy(bsend.at[p, most], back.at[p, most], bs_sem.at[p]).wait()
-        pltpu.make_async_copy(bsend.at[p, me], back.at[p, me], bl_sem.at[p]).wait()
-        pltpu.make_async_copy(bsend.at[p, most], back.at[p, most], br_sem.at[p]).wait()
-
-
-def put_back(parts, out):
-    order = gather_rows(True)
-    for p in range(PIECES):
-        rows = parts[p].reshape(GROUP * MSG, W)
-        moved = jnp.dot(order, rows, preferred_element_type=F32).astype(BF16)
-        out[:, 0, :, p * W : (p + 1) * W] = moved.reshape(ROWS, MSG, W)
 
 
 def on_device(ensemble_obs, obs_values, obs_index, obs_count, loc_weight, state):
     any_space = pl.BlockSpec(memory_space=pl.ANY)
-    vmem = pl.BlockSpec(memory_space=pltpu.VMEM)
-    smem = pl.BlockSpec(memory_space=pltpu.SMEM)
+    vmem = pltpu.VMEM
     dma = pltpu.SemaphoreType.DMA
-    back = pl.pallas_call(
+
+    def in_hbm(array):
+        return pltpu.with_memory_space_constraint(array, pltpu.HBM)
+
+    return pl.pallas_call(
         exchange,
         name="exchange",
-        out_shape=jax.ShapeDtypeStruct((PIECES, PEERS, MSG, W), BF16),
-        in_specs=[any_space, vmem, vmem, vmem, smem, vmem],
-        out_specs=any_space,
+        out_shape=vmem(state.shape, BF16),
+        in_specs=[any_space] * 6,
+        out_specs=pl.BlockSpec(memory_space=vmem),
         scratch_shapes=[
-            pltpu.VMEM((ROWS, PEERS * BLKS, CELLS), BF16),
-            pltpu.VMEM((PIECES, PEERS, MSG, W), BF16),
-            pltpu.VMEM((PIECES, PEERS, MSG, W), BF16),
-            pltpu.VMEM((PIECES, PEERS, MSG, W), BF16),
-            pltpu.VMEM((PEERS, MSG, RIM), BF16),
-            pltpu.VMEM((PEERS, MSG, RIM), BF16),
-            pltpu.VMEM((2, K + 16, RIM), BF16),
-            pltpu.VMEM((2, K + 16, RIM), BF16),
-            pltpu.VMEM((K, POOL), BF16),
-            pltpu.VMEM((BLKS, K, POOL), BF16),
-            pltpu.VMEM((3, K, K), F32),
-            pltpu.VMEM((BLKS, K, POOL), BF16),
-            pltpu.VMEM((PEERS, MSG, POOL), F32),
-            pltpu.VMEM((BLKS * K, BLKS * K), BF16),
-            pltpu.VMEM((BLKS * K, W), BF16),
-            dma((PIECES,)), dma((PIECES,)), dma((PIECES,)), dma((PIECES,)),
-            dma((PIECES,)), dma((PIECES,)), dma((PIECES,)),
+            vmem((ROWS, PEERS * 2 * RIM), BF16),
+            vmem((2, 2 * RIM), BF16),
+            vmem((BLKS, 512), jnp.int32),
+            vmem((BLKS, 512), F32),
+            pltpu.SMEM((1, BLKS), jnp.int32),
+            vmem((ROWS, PEERS * BLKS, CELLS), BF16),
+            vmem((PIECES, PEERS, MSG, W), BF16),
+            vmem((PIECES, PEERS, MSG, W), BF16),
+            vmem((PIECES, PEERS, MSG, W), BF16),
+            vmem((PIECES, PEERS, MSG, W), BF16),
+            vmem((PEERS, MSG, RIM), BF16),
+            vmem((PEERS, MSG, RIM), BF16),
+            vmem((2, K + 16, RIM), BF16),
+            vmem((2, K + 16, RIM), BF16),
+            vmem((K, POOL), BF16),
+            vmem((BLKS, K, POOL), BF16),
+            vmem((3, K, K), F32),
+            vmem((BLKS, K, POOL), BF16),
+            vmem((PEERS, MSG, POOL), F32),
+            vmem((BLKS * K, BLKS * K), BF16),
+            vmem((BLKS * K, W), BF16),
+            dma((5,)), dma((PIECES,)), dma((PIECES,)), dma((PIECES,)), dma((PIECES,)),
+            dma((PIECES,)), dma((PIECES, GROUPS)),
             dma, dma, dma, dma((2,)), dma((2,)),
         ],
         compiler_params=pltpu.CompilerParams(
-            collective_id=0, has_side_effects=True, vmem_limit_bytes=56 << 20
+            collective_id=0, has_side_effects=True, vmem_limit_bytes=48 << 20
         ),
     )(
-        state,
-        ensemble_obs.reshape(ROWS, PEERS * 2 * RIM),
-        obs_values.reshape(2, 2 * RIM),
-        obs_index.reshape(BLKS, 512),
-        obs_count,
-        loc_weight.reshape(BLKS, 512),
+        in_hbm(state),
+        in_hbm(ensemble_obs.reshape(ROWS, PEERS * 2 * RIM)),
+        in_hbm(obs_values.reshape(2, 2 * RIM)),
+        in_hbm(obs_index.reshape(BLKS, 512)),
+        in_hbm(obs_count),
+        in_hbm(loc_weight.reshape(BLKS, 512)),
     )
-    return pl.pallas_call(
-        put_back,
-        name="put_back",
-        grid=(GROUPS,),
-        out_shape=jax.ShapeDtypeStruct(state.shape, BF16),
-        in_specs=[pl.BlockSpec((PIECES, GROUP, MSG, W), lambda g: (0, g, 0, 0))],
-        out_specs=pl.BlockSpec((ROWS, 1, MSG, CELLS), lambda g: (0, 0, g, 0)),
-    )(back)
 
 
 def solution(mesh):

time: 214 us -> 207 us (0.967)
  Pallas kernels: 214 us -> 205 us
    pallas_call x2 -> x1, Pallas kernels: 214 us -> 205 us  [on_device(): pl.pallas_call(exchange, name='exchange', out_shape=vmem(state.shape, BF1...]
where the time goes in v1:
time: 207 us
  Pallas kernels  205 us (99%)
    pallas_call x1, Pallas kernels, on_device(): pl.pallas_call(exchange, name='exchange', out_shape=vmem(state.shape, BF1...  205 us

profile of v1, /device:TPU:1, one launch (start us, length us, event | category | flops | bytes accessed | tf_op | source)
XLA Modules:
  0.0 207.3 jit_solution(12214036227513628256)
XLA Ops:
  0.0 205.3 %exchange.1 = bf16[8,1,128,2048]{3,2,1,0:T(8,128)(2,1)S(1)} custom-call(bf16[8,1,128,2048]{3,2,1,0:T(8,128)(2,1)} %state.1, bf16[8,32768]{1,0:T(8,128)(2,1)} %bitcast.4, bf16[2,512]{1,0:T(2,128)(2,1)} %bitcast.7, s32[2,512]{1,0:T(2,128)} %bitcast.5, s32[1,2]{1,0:T(1,128)} %cnt_in.1, f32[2,512]{1,0:T(2,128)} %bitcast.6), custom_call_target="tpu_custom_call" | custom-call | tf_op jit(solution)/shard_map/exchange/pallas_call | solution.py:354
  205.3 2.0 copy.8

commit v2 on v1

--- a/solution.py
+++ b/solution.py
@@ -66,7 +66,7 @@
     obs, vals, idx, loc, cnt, stage, fsend, frecv, bsend, back, osend, orecv, hsend, hrecv,
     pert, wgt, mats, expand, tbigf, tbig, spert,
     in_sem, st_sem, fs_sem, fr_sem, fl_sem, bs_sem, br_sem,
-    os_sem, or_sem, ol_sem, hs_sem, hr_sem,
+    os_sem, or_sem, ol_sem, hs_sem, hr_sem, relay,
 ):
     me = lax.axis_index("member")
     slab = lax.axis_index("slab")
@@ -75,13 +75,23 @@
 
     barrier = pltpu.get_barrier_semaphore()
 
-    def greet(i, carry):
+    corner = [
+        lax.rem(me // 16 + n // 2, 4) * 16 + lax.rem(me + n, 2) for n in range(8)
+    ]
+
+    def plane(dz):
+        at = lax.rem(me // 2 + dz, 8) * 2
+        return [corner[n] + at for n in range(8)]
+
+    up, down = plane(1)[0], plane(7)[0]
+
+    def signal(semaphore, member):
         pl.semaphore_signal(
-            barrier, inc=1, device_id={"member": lax.rem(me + 27 * i, PEERS)}, device_id_type=MESH
+            semaphore, inc=1, device_id={"member": member}, device_id_type=MESH
         )
-        return carry
-
-    lax.fori_loop(1, PEERS, greet, 0, unroll=7)
+
+    for d in plane(1) + plane(7) + plane(0)[1:]:
+        signal(barrier, d)
     for neighbour in (left, right):
         pl.semaphore_signal(barrier, inc=1, device_id={"slab": neighbour}, device_id_type=MESH)
 
@@ -103,23 +113,32 @@
     for p in range(PIECES):
         stage_copy(p).start()
     fetches[0].wait()
-    pl.semaphore_wait(barrier, PEERS - 1 + 2)
+    pl.semaphore_wait(barrier, 8 + 8 + 7 + 2)
 
     def message(r):
         a = obs[:, pl.ds(pl.multiple_of(r * 2 * RIM, 2 * RIM), RIM)].astype(F32)
         b = obs[:, pl.ds(pl.multiple_of(r * 2 * RIM + RIM, RIM), RIM)].astype(F32)
         osend[r] = jnp.concatenate([a, b], axis=0).astype(BF16)
 
-    def send_obs(i, carry):
-        d = lax.rem(me + 27 * i, PEERS)
+    def send_obs(d):
         message(d)
         pltpu.make_async_remote_copy(
             src_ref=osend.at[d], dst_ref=orecv.at[me], send_sem=os_sem, recv_sem=or_sem,
             device_id={"member": d}, device_id_type=MESH,
         ).start()
-        return carry
-
-    lax.fori_loop(1, PEERS, send_obs, 0)
+
+    for far in range(1, 5):
+        if far in (2, 3):
+            pl.semaphore_wait(relay.at[far - 2, 0], 1)
+        if far > 1:
+            pl.semaphore_wait(relay.at[far - 2, 1], 1)
+        if far < 4:
+            signal(relay.at[far - 1, 1], up)
+        if far < 3:
+            signal(relay.at[far - 1, 0], down)
+        reach = {1: plane(1) + plane(7), 4: plane(4)}.get(far, plane(far) + plane(8 - far))
+        for d in reach + (plane(0)[1:] if far == 1 else []):
+            send_obs(d)
     message(me)
     own_obs = pltpu.make_async_copy(osend.at[me], orecv.at[me], ol_sem)
     own_obs.start()
@@ -381,7 +400,7 @@
             vmem((BLKS * K, W), BF16),
             dma((5,)), dma((PIECES,)), dma((PIECES,)), dma((PIECES,)), dma((PIECES,)),
             dma((PIECES,)), dma((PIECES, GROUPS)),
-            dma, dma, dma, dma((2,)), dma((2,)),
+            dma, dma, dma, dma((2,)), dma((2,)), pltpu.SemaphoreType.REGULAR((3, 2)),
         ],
         compiler_params=pltpu.CompilerParams(
             collective_id=0, has_side_effects=True, vmem_limit_bytes=48 << 20

time: 207 us -> 206 us (level)
  no operation moved by 1% of the time
where the time goes in v2:
time: 206 us
  Pallas kernels  204 us (99%)
    pallas_call x1, Pallas kernels, on_device(): pl.pallas_call(exchange, name='exchange', out_shape=vmem(state.shape, BF1...  204 us

profile of v2, /device:TPU:1, one launch (start us, length us, event | category | flops | bytes accessed | tf_op | source)
XLA Modules:
  0.0 206.2 jit_solution(6504790070684222864)
XLA Ops:
  0.0 204.2 %exchange.1 = bf16[8,1,128,2048]{3,2,1,0:T(8,128)(2,1)S(1)} custom-call(bf16[8,1,128,2048]{3,2,1,0:T(8,128)(2,1)} %state.1, bf16[8,32768]{1,0:T(8,128)(2,1)} %bitcast.4, bf16[2,512]{1,0:T(2,128)(2,1)} %bitcast.7, s32[2,512]{1,0:T(2,128)} %bitcast.5, s32[1,2]{1,0:T(1,128)} %cnt_in.1, f32[2,512]{1,0:T(2,128)} %bitcast.6), custom_call_target="tpu_custom_call" | custom-call | tf_op jit(solution)/shard_map/exchange/pallas_call | solution.py:373
  204.2 2.0 copy.8

commit v3 on v2

--- a/solution.py
+++ b/solution.py
@@ -314,7 +314,7 @@
         lax.fori_loop(0, 16, less_mean, 0)
 
         def apply(i, carry):
-            part = lax.rem(me // 16 + i, 4)
+            part = lax.rem(me // 16 + 1 + i, 4)
             rows = tbig[pl.ds(pl.multiple_of(part * 256, 256), 256)]
             moved = jnp.dot(rows, spert[...], preferred_element_type=F32)
             new = moved.reshape(16, MSG, W) + mean[None]
@@ -322,7 +322,9 @@
             bsend[p, pl.ds(first, 16)] = new.astype(BF16)
 
             def one(j, inner):
-                d = first + lax.rem(j * 7 + me, 16)
+                step = j // 2
+                dz = lax.rem(4 + (1 - 2 * lax.rem(step, 2)) * ((step + 1) // 2) + 8, 8)
+                d = first + lax.rem(me // 2 + dz, 8) * 2 + lax.rem(j + me, 2)
 
                 @pl.when(d != me)
                 def _():
@@ -343,7 +345,7 @@
     for p in range(PIECES):
 
         def place(i, carry):
-            y = lax.rem(me // 16 + 4 - i // 2, 4)
+            y = lax.rem(me // 16 + 3 - i // 2, 4)
             g = y * 2 + lax.rem(i, 2)
             some = pl.ds(pl.multiple_of(g * GROUP, GROUP), GROUP)
             pltpu.make_async_copy(bsend.at[p, some], back.at[p, some], br_sem.at[p, g]).wait()

time: 206 us -> 206 us (level)
  no operation moved by 1% of the time
where the time goes in v3:
time: 206 us; the launch traced here: 205 us
  Pallas kernels  203 us (99%)
    pallas_call x1, Pallas kernels, on_device(): pl.pallas_call(exchange, name='exchange', out_shape=vmem(state.shape, BF1...  203 us

profile of v3, /device:TPU:1, one launch (start us, length us, event | category | flops | bytes accessed | tf_op | source)
XLA Modules:
  0.0 205.4 jit_solution(7228106888262946178)
XLA Ops:
  0.0 203.4 %exchange.1 = bf16[8,1,128,2048]{3,2,1,0:T(8,128)(2,1)S(1)} custom-call(bf16[8,1,128,2048]{3,2,1,0:T(8,128)(2,1)} %state.1, bf16[8,32768]{1,0:T(8,128)(2,1)} %bitcast.4, bf16[2,512]{1,0:T(2,128)(2,1)} %bitcast.7, s32[2,512]{1,0:T(2,128)} %bitcast.5, s32[1,2]{1,0:T(1,128)} %cnt_in.1, f32[2,512]{1,0:T(2,128)} %bitcast.6), custom_call_target="tpu_custom_call" | custom-call | tf_op jit(solution)/shard_map/exchange/pallas_call | solution.py:375
  203.4 2.0 copy.8

commit v4 on v3

--- a/solution.py
+++ b/solution.py
@@ -19,7 +19,7 @@
 BLKS = 2
 MSG = BLKS * ROWS
 CELLS = 2048
-PIECES = 4
+PIECES = 2
 W = CELLS // PIECES
 RIM = 256
 POOL = 1024

time: 206 us -> 206 us (level)
  no operation moved by 1% of the time
where the time goes in v4:
time: 206 us
  Pallas kernels  204 us (99%)
    pallas_call x1, Pallas kernels, on_device(): pl.pallas_call(exchange, name='exchange', out_shape=vmem(state.shape, BF1...  204 us

profile of v4, /device:TPU:1, one launch (start us, length us, event | category | flops | bytes accessed | tf_op | source)
XLA Modules:
  0.0 205.9 jit_solution(13776839477730402936)
XLA Ops:
  0.0 203.9 %exchange.1 = bf16[8,1,128,2048]{3,2,1,0:T(8,128)(2,1)S(1)} custom-call(bf16[8,1,128,2048]{3,2,1,0:T(8,128)(2,1)} %state.1, bf16[8,32768]{1,0:T(8,128)(2,1)} %bitcast.4, bf16[2,512]{1,0:T(2,128)(2,1)} %bitcast.7, s32[2,512]{1,0:T(2,128)} %bitcast.5, s32[1,2]{1,0:T(1,128)} %cnt_in.1, f32[2,512]{1,0:T(2,128)} %bitcast.6), custom_call_target="tpu_custom_call" | custom-call | tf_op jit(solution)/shard_map/exchange/pallas_call | solution.py:375
  203.9 2.0 copy.8
